TPU v7x, 128 devices: a whole 4x4x4 slice. The times are simulated.
128 devices in a mesh: rows: 8 (over z, core), cache: 16 (over x, y).
Axes of the slice: x: 4, y: 4, z: 4, core: 2. Of those that a mesh axis runs over, the one named last changes fastest.
Arguments:
- queries: bfloat16 [32, 128, 576], P('rows', 'cache'), may hold values from -20 to 20
- prefix_cache: bfloat16 [256, 1024, 576], P(('rows', 'cache')), may hold values from -12 to 12
- suffix_cache: bfloat16 [32, 1024, 576], P('rows'), may hold values from -12 to 12
- suffix_len: int32 [32], P('rows'), may hold values from 2 to 1024, as said below
- touch_mask: int32 [32, 256], replicated, may hold values from 0 to 1, as said below
- block_slot: int32 [256], replicated, may hold values from 0 to 255, as said below
Outputs:
- latent_out: bfloat16 [32, 128, 512], P('rows', 'cache')
- lse_out: float32 [32, 128], P('rows', 'cache')
Inputs may be any that keep to these rules, and one draw needn't show every extreme that they name: `suffix_len`: some request has exactly 1024 suffix tokens. `touch_mask`: each request touches 4 to 16 logical blocks; some request touches exactly 4 and some exactly 16. Within each aligned block of 4 requests, at most 2 requests read blocks held by any one holder, and in every such block some holder is read by exactly 2 of them. `block_slot`: each slot holds exactly one logical block.
All inputs are finite; a program needn't handle non-finite values.
Results may differ from a plain program's by a relative error of at most 0.0048.
Values may be sent and summed in bfloat16 or wider, within the bound.
No kernel may reach another device: no remote copies, remote signals or barrier semaphores. Data moves between devices by JAX's collectives and lax.ppermute only.
A program may use at most 64 MiB of HBM per device.

v0:
```python
import functools
import jax
import jax.numpy as jnp
from jax import lax
from jax.experimental import pallas as pl
from jax.experimental.pallas import tpu as pltpu
from jax.sharding import Mesh, PartitionSpec as P

H = 128
LAT = 512
DK = 576
BLK = 1024
BLK_DEV = 2
SUF = 1024
DEVS = 128
SIDE = 2
ROWS = 8 // SIDE
SEND = SIDE * DK
PACK = SIDE * LAT + 128
GROUPS = 8
GROUP_ROWS = 128

SOFTMAX_SCALE = 192.0 ** (-0.5)
MASKED_SCORE = -1e30
BF = jnp.bfloat16
F32 = jnp.float32
MIB = 1024 * 1024


def iota(shape, dim):
    return lax.broadcasted_iota(jnp.int32, shape, dim)


def ones_where(mask):
    return jnp.where(mask, 1.0, 0.0).astype(BF)


def dot(a, b, ca=1, cb=0):
    return lax.dot_general(a, b, (((ca,), (cb,)), ((), ())), preferred_element_type=F32)


def route_kernel(offset, me_ref, q_ref, touch_ref, slot_ref, send_ref, route_ref, table_ref):
    me = me_ref[0]
    group = lax.shift_right_logical(me, 4)
    n = DEVS * ROWS
    chips = DEVS // 2
    touch = touch_ref[...].astype(F32).astype(BF)
    reqs, blocks = touch.shape
    slots = slot_ref[...]
    chip_of = lax.shift_right_logical(slots, 6) * 16 + (lax.shift_right_logical(slots, 1) & 15)
    chip_touch = dot(ones_where(iota((chips, blocks), 0) == chip_of), touch, 1, 1)
    chip_touch = jnp.minimum(chip_touch, 1.0)
    of_group = lax.shift_right_logical(iota((reqs, reqs), 0), 2)
    before = ones_where(
        (of_group == lax.shift_right_logical(iota((reqs, reqs), 1), 2)) & (iota((reqs, reqs), 0) < iota((reqs, reqs), 1))
    )
    rank = dot(chip_touch.astype(BF), before)
    mine = ones_where(iota((reqs, 32), 0) == group * 4 + lax.shift_right_logical(iota((reqs, 32), 1), 3))
    first = ((group & 1) + offset).astype(F32)
    second = ((1 - (group & 1)) + offset).astype(F32)
    by_core = [jnp.where(rank == want, chip_touch, 0.0) for want in (first, second)]
    by_dev = [by_core[k][z * 16 : z * 16 + 16] for z in range(4) for k in (0, 1)]
    by_dev = dot(jnp.concatenate(by_dev, axis=0).astype(BF), mine)
    chosen = jnp.broadcast_to(by_dev[:, None, :], (DEVS, ROWS, 32)).reshape(n, 32)
    in_row = (iota((n, 32), 1) & 7) // SIDE == (iota((n, 32), 0) & (ROWS - 1))
    chosen = jnp.where(in_row, chosen, 0.0)
    route_ref[...] = chosen.astype(BF)
    by_place, spread = [], []
    q = q_ref[...].astype(F32)
    for j in range(SIDE):
        by_place.append(jnp.where((iota((n, 32), 1) & (SIDE - 1)) == j, chosen, 0.0))
        pieces = [jnp.zeros((32, j * LAT), F32), q[:, :LAT], jnp.zeros((32, (SIDE - 1 - j) * LAT), F32)]
        pieces += [jnp.zeros((32, j * (DK - LAT)), F32), q[:, LAT:], jnp.zeros((32, (SIDE - 1 - j) * (DK - LAT)), F32)]
        spread.append(jnp.concatenate([piece for piece in pieces if piece.shape[1]], axis=1))
    by_place = jnp.concatenate(by_place, axis=1).astype(BF)
    spread = jnp.concatenate(spread, axis=0).astype(BF)
    send_ref[...] = dot(by_place, spread).astype(BF).reshape(send_ref.shape)
    core = lax.shift_right_logical(me, 4) & 1
    b = iota((8, blocks), 0)
    owner = jnp.where(b < 2, me, me ^ 16)
    wanted = jnp.where(b < 4, owner * 2 + (b & 1), -1)
    block_touch = dot(ones_where(slots == wanted), touch, 1, 1)
    any_touch = jnp.max(block_touch, axis=0, keepdims=True)
    any_touch = jnp.broadcast_to(any_touch, (8, reqs))
    place = dot(any_touch.astype(BF), before)
    served = (core ^ (lax.shift_right_logical(iota((8, reqs), 1), 2) & 1)) + offset
    in_group = ones_where(lax.shift_right_logical(iota((reqs, 128), 0), 2) == iota((reqs, 128), 1))
    bits = dot(jnp.where(place == served.astype(F32), block_touch, 0.0).astype(BF), in_group)
    most = dot(chip_touch.astype(BF), in_group)
    most = jnp.max(jnp.max(most, axis=0, keepdims=True), axis=1, keepdims=True)
    table_ref[...] = jnp.where(iota((8, 128), 0) == 7, most, bits).astype(jnp.int32)


def route(offset, me, q_rows, touch_mask, block_slot):
    n = DEVS * ROWS
    vmem = pl.BlockSpec(memory_space=pltpu.VMEM)
    return pl.pallas_call(
        functools.partial(route_kernel, offset),
        out_shape=(
            jax.ShapeDtypeStruct((DEVS, ROWS, SEND), BF),
            jax.ShapeDtypeStruct((n, 32), BF),
            jax.ShapeDtypeStruct((8, 128), jnp.int32),
        ),
        in_specs=[pl.BlockSpec(memory_space=pltpu.SMEM), vmem, vmem, vmem],
        out_specs=(vmem, vmem, vmem),
        compiler_params=pltpu.CompilerParams(vmem_limit_bytes=32 * MIB),
        cost_estimate=pl.CostEstimate(flops=2 * n * 32 * 1024, bytes_accessed=2 * n * SEND, transcendentals=0),
        name="route",
    )(me, q_rows, touch_mask, block_slot.reshape(1, -1))


LOG2_E = 1.4426950408889634
LN_2 = 0.6931471805599453


def holder_kernel(table_ref, packets_ref, own_ref, far_ref, out_ref, peer_ref, q, top, total, acc, out, todo, out_sems, peer_sem):
    fetch = pltpu.make_async_copy(far_ref, peer_ref, peer_sem)
    fetch.start()
    share = 16 * ROWS
    for g in range(GROUPS):
        x = packets_ref[g * 16 : g * 16 + 16].reshape(share, SEND)
        for j in range(SIDE):
            here = slice(j * share, j * share + share)
            q[g, here, :LAT] = x[:, j * LAT : j * LAT + LAT]
            rotary = SIDE * LAT + j * (DK - LAT)
            q[g, here, LAT:] = x[:, rotary : rotary + DK - LAT]
    counts = []
    for b in range(4):
        count = jnp.int32(0)
        for g in range(GROUPS):
            todo[b, count] = g
            count = count + jnp.where(table_ref[b, g] > 0, 1, 0)
        todo[b, count] = GROUPS
        counts.append(count)
    top[...] = jnp.full(top.shape, MASKED_SCORE, F32)
    total[...] = jnp.ones(total.shape, F32)
    acc[...] = jnp.zeros(acc.shape, F32)
    def work(ref, units):
        c = SOFTMAX_SCALE * LOG2_E
        scores = []
        for block, pair in units:
            rows = jnp.concatenate([q[jnp.minimum(g, GROUPS - 1)] for g in pair], axis=0)
            scores.append(dot(rows, ref[block]))
        for s, (block, pair) in zip(scores, units):
            old = jnp.concatenate([top[g] for g in pair], axis=0)
            new = jnp.maximum(old, jnp.max(s, axis=1, keepdims=True) * c)
            scale = jnp.exp2(old - new)
            p = jnp.exp2(s * c - new)
            added = jnp.sum(p, axis=1, keepdims=True)
            value = dot(p.astype(BF), ref[block, :LAT, :], 1, 1)
            for k, g in enumerate(pair):
                here = slice(k * GROUP_ROWS, (k + 1) * GROUP_ROWS)
                top[g] = new[here]
                total[g] = total[g] * scale[here] + added[here]
                acc[g] = acc[g] * scale[here] + value[here]

    for half, ref in enumerate((own_ref, peer_ref)):
        if half == 1:
            fetch.wait()
        pairs = [lax.shift_right_logical(counts[2 * half + k] + 1, 1) for k in (0, 1)]
        n = pairs[0] + pairs[1]

        def unit(u, half=half, pairs=pairs):
            block = jnp.where(u < pairs[0], 0, 1)
            i = 2 * (u - block * pairs[0])
            return block, [todo[2 * half + block, i], todo[2 * half + block, i + 1]]

        def step(i, carry, ref=ref, unit=unit):
            work(ref, [unit(2 * i), unit(2 * i + 1)])
            return carry

        lax.fori_loop(0, lax.shift_right_logical(n, 1), step, 0)

        @pl.when((n & 1) == 1)
        def _(ref=ref, unit=unit, n=n):
            work(ref, [unit(n - 1)])

    copies = []
    for g in range(GROUPS):
        value = acc[g] * (1.0 / total[g])
        lse = (top[g] + jnp.log2(total[g])) * LN_2
        high = lse.astype(BF).astype(F32)
        middle = (lse - high).astype(BF).astype(F32)
        low = lse - high - middle
        lane = iota((share, 128), 1)
        tail = jnp.where(lane == 3 * SIDE, 1.0, 0.0)
        for j in range(SIDE):
            for k, piece in enumerate((high, middle, low)):
                tail = jnp.where(lane == 3 * j + k, piece[j * share : j * share + share], tail)
        row = [value[j * share : j * share + share] for j in range(SIDE)] + [tail]
        row = jnp.concatenate(row, axis=1).astype(BF)
        here = pl.ds(g * 16, 16)
        out[here] = row.reshape(16, ROWS, PACK)
        copies.append(pltpu.make_async_copy(out.at[here], out_ref.at[here], out_sems.at[g]))
        copies[-1].start()
    for copy in copies:
        copy.wait()


def holder(table, queries, own, peer):
    vmem = pl.BlockSpec(memory_space=pltpu.VMEM)
    return pl.pallas_call(
        holder_kernel,
        out_shape=jax.ShapeDtypeStruct((DEVS, ROWS, PACK), BF),
        in_specs=[pl.BlockSpec(memory_space=pltpu.SMEM), vmem, vmem, pl.BlockSpec(memory_space=pl.ANY)],
        out_specs=pl.BlockSpec(memory_space=pl.ANY),
        scratch_shapes=[
            pltpu.VMEM((BLK_DEV, DK, BLK), BF),
            pltpu.VMEM((GROUPS, GROUP_ROWS, DK), BF),
            pltpu.VMEM((GROUPS + 1, GROUP_ROWS, 1), F32),
            pltpu.VMEM((GROUPS + 1, GROUP_ROWS, 1), F32),
            pltpu.VMEM((GROUPS + 1, GROUP_ROWS, LAT), F32),
            pltpu.VMEM((DEVS, ROWS, PACK), BF),
            pltpu.SMEM((4, 16), jnp.int32),
            pltpu.SemaphoreType.DMA((GROUPS,)),
            pltpu.SemaphoreType.DMA,
        ],
        compiler_params=pltpu.CompilerParams(vmem_limit_bytes=32 * MIB),
        cost_estimate=pl.CostEstimate(
            flops=2 * 1024 * 1024 * (DK + LAT), bytes_accessed=4 * 2 * BLK * DK, transcendentals=1024 * 1024
        ),
        name="holder",
    )(table, queries, own, peer)


def suffix_kernel(len_ref, q_ref, kv_ref, out_ref, lse_ref):
    r = pl.program_id(0)
    kv = kv_ref[0]
    s = dot(q_ref[0], kv) * SOFTMAX_SCALE
    s = jnp.where(iota(s.shape, 1) < len_ref[r], s, MASKED_SCORE)
    top = jnp.max(s, axis=1, keepdims=True)
    p = jnp.exp(s - top)
    total = jnp.sum(p, axis=1, keepdims=True)
    out_ref[0] = dot(p.astype(BF), kv[:LAT], 1, 1) / total
    lse_ref[0] = jnp.broadcast_to(top + jnp.log(total), lse_ref.shape[1:])


def suffix(lengths, queries, cache):
    reqs, heads, _ = queries.shape
    return pl.pallas_call(
        suffix_kernel,
        grid=(reqs,),
        out_shape=(
            jax.ShapeDtypeStruct((reqs, heads, LAT), F32),
            jax.ShapeDtypeStruct((reqs, heads, 128), F32),
        ),
        in_specs=[
            pl.BlockSpec(memory_space=pltpu.SMEM),
            pl.BlockSpec((1, heads, DK), lambda r: (r, 0, 0)),
            pl.BlockSpec((1, DK, SUF), lambda r: (r, 0, 0)),
        ],
        out_specs=(
            pl.BlockSpec((1, heads, LAT), lambda r: (r, 0, 0)),
            pl.BlockSpec((1, heads, 128), lambda r: (r, 0, 0)),
        ),
        compiler_params=pltpu.CompilerParams(vmem_limit_bytes=32 * MIB),
        cost_estimate=pl.CostEstimate(
            flops=2 * 4 * 256 * 1024 * (DK + LAT), bytes_accessed=4 * 2 * SUF * DK, transcendentals=4 * 8 * 1024
        ),
        name="suffix",
    )(lengths, queries, cache)


def merge_kernel(rounds, *refs):
    parts, routes = refs[:rounds], refs[rounds : 2 * rounds]
    suffix_ref, suffix_lse_ref, out_ref, lse_ref = refs[2 * rounds :]
    heads = 32
    eye = iota((heads, heads), 0) == iota((heads, heads), 1)
    suffix_lse = suffix_lse_ref[:, :1]
    ceiling = jnp.max(jnp.where(eye, suffix_lse, MASKED_SCORE), axis=0, keepdims=True)
    scores = []
    n = DEVS * ROWS
    flat = [part[...].reshape(n, PACK) for part in parts]
    place = iota((n, heads), 1) & (SIDE - 1)
    for part, chosen in zip(flat, routes):
        tail = part[:, SIDE * LAT :].astype(F32)
        score = MASKED_SCORE
        for j in range(SIDE):
            lse = tail[:, 3 * j : 3 * j + 1] + tail[:, 3 * j + 1 : 3 * j + 2] + tail[:, 3 * j + 2 : 3 * j + 3]
            score = jnp.where(place == j, lse, score)
        score = jnp.where(chosen[...] > 0.5, score, MASKED_SCORE)
        scores.append(score)
        ceiling = jnp.maximum(ceiling, jnp.max(score, axis=0, keepdims=True))
    top = jnp.max(jnp.where(eye, ceiling, MASKED_SCORE), axis=1, keepdims=True)
    weight = jnp.exp(suffix_lse - top)
    merged = weight * suffix_ref[...]
    total = weight
    place = iota((heads, LAT), 0) & (SIDE - 1)
    for part, score in zip(flat, scores):
        w = jnp.exp(score - ceiling)
        high = w.astype(BF)
        low = (w - high.astype(F32)).astype(BF)
        both = jnp.concatenate([high, low], axis=1).T
        sums = dot(both, part)
        sums = sums[:heads] + sums[heads:]
        total = total + sums[:, SIDE * LAT + 3 * SIDE : SIDE * LAT + 3 * SIDE + 1]
        for j in range(SIDE):
            merged = merged + jnp.where(place == j, sums[:, j * LAT : j * LAT + LAT], 0.0)
    out = (merged / total).astype(BF)
    lse = top + jnp.log(total)
    diagonal = iota((8, 8), 0) == iota((8, 8), 1)
    for q in range(4):
        out_ref[q] = out[q * 8 : q * 8 + 8]
        column = jnp.where(diagonal, lse[q * 8 : q * 8 + 8], 0.0)
        lse_ref[q : q + 1, :] = jnp.sum(column, axis=0, keepdims=True)


def merge(parts, routes, suffix_out, suffix_lse):
    vmem = pl.BlockSpec(memory_space=pltpu.VMEM)
    return pl.pallas_call(
        functools.partial(merge_kernel, len(parts)),
        out_shape=(jax.ShapeDtypeStruct((4, 8, LAT), BF), jax.ShapeDtypeStruct((4, 8), F32)),
        in_specs=[vmem] * (2 * len(parts) + 2),
        out_specs=(vmem, vmem),
        compiler_params=pltpu.CompilerParams(vmem_limit_bytes=32 * MIB),
        name="merge",
    )(*parts, *routes, suffix_out, suffix_lse)


AXES = ("z", "core", "x", "y")


def on_device(queries, prefix_cache, suffix_cache, suffix_len, touch_mask, block_slot):
    reqs, heads, _ = queries.shape
    me = lax.axis_index(AXES).astype(jnp.int32).reshape(1)
    q_rows = queries.reshape(reqs * heads, DK)
    own = prefix_cache.transpose(0, 2, 1)
    peer = lax.ppermute(own, "core", [(0, 1), (1, 0)])

    def one_round(offset, peer):
        send, chosen, table = route(offset, me, q_rows, touch_mask, block_slot)
        got = lax.all_to_all(send, AXES, split_axis=0, concat_axis=0, tiled=True)
        parts = holder(table, got, own, peer)
        parts = lax.all_to_all(parts, AXES, split_axis=0, concat_axis=0, tiled=True)
        return parts, chosen, table

    parts, chosen, table = one_round(0, peer)
    suffix_out, suffix_lse = suffix(suffix_len, queries, suffix_cache.transpose(0, 2, 1))
    suffix_out = suffix_out.reshape(reqs * heads, LAT)
    suffix_lse = suffix_lse.reshape(reqs * heads, 128)

    def one(parts, chosen, peer):
        return merge([parts], [chosen], suffix_out, suffix_lse)

    def two(parts, chosen, peer):
        more, more_chosen, _ = one_round(2, peer)
        return merge([parts, more], [chosen, more_chosen], suffix_out, suffix_lse)

    return tuple(lax.cond(table[7, 0] > 2, two, one, parts, chosen, peer))


def solution(mesh):
    grid = Mesh(mesh.devices.reshape(4, 2, 4, 4), AXES)
    rows, cache = ("z", "core"), ("x", "y")
    in_specs = (
        P(rows, cache, None),
        P(AXES, None, None),
        P(rows, None, None),
        P(rows),
        P(),
        P(),
    )
    out_specs = (P(rows, cache, None), P(rows, cache))
    return jax.shard_map(
        on_device, mesh=grid, in_specs=in_specs, out_specs=out_specs, check_vma=False
    )
```

profile of v0, /device:TPU:0, one launch (start us, length us, event | category | flops | bytes accessed | tf_op | source)
XLA Modules:
  0.0 69.6 jit_solution(910065274941053605)
XLA Ops:
  0.6 0.1 collective-permute-start
  0.7 2.0 %route.3 = (bf16[128,4,1152]{2,1,0:T(4,128)(2,1)S(1)}, bf16[512,32]{1,0:T(8,128)(2,1)S(1)}, s32[8,128]{1,0:T(8,128)S(1)}) custom-call(s32[1]{0:T(128)} %bitcast.1.me_ref, bf16[32,576]{1,0:T(8,128)(2,1)} %bitcast.17, s32[32,256]{1,0:T(8,128)} %touch_ref.1, s32[1,256]{1,0:T(1,128)} %bitcast.19), custom_call_target="tpu_custom_call" | custom-call | flops 33554432 | bytes 1179648 | tf_op jit(solution)/shard_map/route/pallas_call | solution.py:97
  2.7 0.0 copy-start.2
  2.7 31.4 %all_to_all.20.packets_ref = bf16[128,4,1152]{2,1,0:T(4,128)(2,1)S(1)} all-to-all(bf16[128,4,1152]{2,1,0:T(4,128)(2,1)S(1)} %get-tuple-element.53), channel_id=1, replica_groups=mesh['z'=4,'core'=2,'x'=4,'y'=4] {'z','core','x','y'}, dimensions={0} | all-to-all | bytes 2359296 | tf_op jit(solution)/shard_map/all_to_all | solution.py:332
  34.2 0.0 collective-permute-done.far_ref
  34.2 0.0 copy-done.2
  34.2 8.6 %holder.3 = bf16[128,4,1152]{2,1,0:T(4,128)(2,1)} custom-call(s32[8,128]{1,0:T(8,128)S(1)} %get-tuple-element.52.table_ref, bf16[128,4,1152]{2,1,0:T(4,128)(2,1)S(1)} %all_to_all.20.packets_ref, bf16[2,576,1024]{2,1,0:T(8,128)(2,1)S(1)} %bitcast.16, bf16[2,576,1024]{2,1,0:T(8,128)(2,1)} %collective-permute-done.far_ref), custom_call_target="tpu_custom_call" | custom-call | flops 2281701376 | bytes 4718592 | tf_op jit(solution)/shard_map/holder/pallas_call | solution.py:202
  42.8 0.0 copy-start.1
  42.8 0.0 copy-start.4
  42.8 4.6 %all-to-all-start.3 = ((bf16[128,4,1152]{2,1,0:T(4,128)(2,1)}), bf16[128,4,1152]{2,1,0:T(4,128)(2,1)S(1)}, u32[]{:S(2)}, u32[]{:S(2)}) async-start(bf16[128,4,1152]{2,1,0:T(4,128)(2,1)} %holder.3), calls=%async_computation.3 | async-start | bytes 2359296 | tf_op jit(solution)/shard_map/all_to_all | solution.py:334
  47.5 0.5 slice.3
  48.6 0.0 copy-done.1
  48.7 0.0 copy-done.4
  48.7 0.0 copy-start
  48.7 2.3 %copy-done = bf16[4,1024,576]{1,2,0:T(8,128)(2,1)S(1)} copy-done((bf16[4,1024,576]{1,2,0:T(8,128)(2,1)S(1)}, bf16[4,1024,576]{1,2,0:T(8,128)(2,1)}, u32[]{:S(2)}) %copy-start) | copy-done | bytes 4718616
  51.0 0.0 copy-start.5
  51.0 0.0 copy-start.6
  51.0 3.3 %suffix.1 = (f32[4,8,512]{2,1,0:T(8,128)S(1)}, f32[4,8,128]{2,1,0:T(8,128)S(1)}) custom-call(s32[4]{0:T(128)S(1)} %copy-done.1, bf16[4,8,576]{2,1,0:T(8,128)(2,1)S(1)} %copy-done.4, bf16[4,576,1024]{2,1,0:T(8,128)(2,1)S(1)} %bitcast.9), custom_call_target="tpu_custom_call" | custom-call | flops 2281701376 | bytes 4718592 | tf_op jit(solution)/shard_map/suffix/pallas_call | solution.py:240
  54.3 13.6 %all-to-all-done.3 = bf16[128,4,1152]{2,1,0:T(4,128)(2,1)S(1)} async-done(((bf16[128,4,1152]{2,1,0:T(4,128)(2,1)}), bf16[128,4,1152]{2,1,0:T(4,128)(2,1)S(1)}, u32[]{:S(2)}, u32[]{:S(2)}) %all-to-all-start.3) | async-done | bytes 1179680 | tf_op jit(solution)/shard_map/all_to_all | solution.py:334
  67.9 0.0 copy-done.5
  67.9 0.0 copy-done.6
  67.9 1.8 %conditional.1 = ((bf16[4,8,512]{2,1,0:T(8,128)(2,1)}, f32[4,8]{1,0:T(4,128)})) conditional(s32[]{:T(128)} %bitcast.4, (bf16[128,4,1152]{2,1,0:T(4,128)(2,1)S(1)}, bf16[512,32]{1,0:T(8,128)(2,1)S(1)}, f32[32,512]{1,0:T(8,128)S(1)}, f32[32,128]{1,0:T(8,128)S(1)}) %tuple.25, (s32[256]{0:T(256)S(1)}, s32[1]{0:T(128)}, bf16[32,576]{1,0:T(8,128)(2,1)S(1)}, ...), branch_computations={%region_0.0_spmd, %region_1.0_spmd} | conditional | flops 2315255808 | bytes 20054052 | solution.py:349
  67.9 1.8 %merge.2 = (bf16[4,8,512]{2,1,0:T(8,128)(2,1)}, f32[4,8]{1,0:T(4,128)}) custom-call(bf16[128,4,1152]{2,1,0:T(4,128)(2,1)S(1)} %get-tuple-element.28.refs_0_, bf16[512,32]{1,0:T(8,128)(2,1)S(1)} %get-tuple-element.29.refs_1_, f32[32,512]{1,0:T(8,128)S(1)} %get-tuple-element.30.refs_2_, f32[32,128]{1,0:T(8,128)S(1)} %get-tuple-element.31.refs_3_), custom_call_target="tpu_custom_call" | custom-call | tf_op jit(solution)/shard_map/cond/branch_0_fun/merge/pallas_call | solution.py:310
Async XLA Ops:
  0.6 33.6 %collective-permute-start = (bf16[2,576,1024]{2,1,0:T(8,128)(2,1)}, bf16[2,576,1024]{2,1,0:T(8,128)(2,1)}, u32[]{:S(2)}, u32[]{:S(2)}) collective-permute-start(bf16[2,576,1024]{2,1,0:T(8,128)(2,1)} %bitcast.14), channel_id=1, source_target_pairs={{0,16},{16,0},{1,17},{17,1},{2,18},{18,2},{3,19},{19,3},{4,20},{20... | collective-permute-start | bytes 7077896 | tf_op jit(solution)/shard_map/ppermute | solution.py:328
  2.7 31.5 %copy-start.2 = (bf16[2,1024,576]{1,2,0:T(8,128)(2,1)S(1)}, bf16[2,1024,576]{1,2,0:T(8,128)(2,1)}, u32[]{:S(2)}) copy-start(bf16[2,1024,576]{1,2,0:T(8,128)(2,1)} %param.9) | copy-start | bytes 7077892
  42.8 5.9 %copy-start.1 = (s32[4]{0:T(128)S(1)}, s32[4]{0:T(128)}, u32[]{:S(2)}) copy-start(s32[4]{0:T(128)} %len_ref.1) | copy-start | bytes 52
  42.8 5.8 %copy-start.4 = (bf16[4,8,576]{2,1,0:T(8,128)(2,1)S(1)}, bf16[4,8,576]{2,1,0:T(8,128)(2,1)}, u32[]{:S(2)}) copy-start(bf16[4,8,576]{2,1,0:T(8,128)(2,1)} %q_ref.1) | copy-start | bytes 110596
  42.8 25.1 %all-to-all-start.3 = ((bf16[128,4,1152]{2,1,0:T(4,128)(2,1)}), bf16[128,4,1152]{2,1,0:T(4,128)(2,1)S(1)}, u32[]{:S(2)}, u32[]{:S(2)}) async-start(bf16[128,4,1152]{2,1,0:T(4,128)(2,1)} %holder.3), calls=%async_computation.3 | async-start | bytes 2359296 | tf_op jit(solution)/shard_map/all_to_all | solution.py:334
  48.7 2.3 %copy-start = (bf16[4,1024,576]{1,2,0:T(8,128)(2,1)S(1)}, bf16[4,1024,576]{1,2,0:T(8,128)(2,1)}, u32[]{:S(2)}) copy-start(bf16[4,1024,576]{1,2,0:T(8,128)(2,1)} %param.10) | copy-start | bytes 14155780
  51.0 16.9 %copy-start.5 = (s32[32,256]{1,0:T(8,128)S(1)}, s32[32,256]{1,0:T(8,128)}, u32[]{:S(2)}) copy-start(s32[32,256]{1,0:T(8,128)} %touch_ref.1) | copy-start | bytes 98308
  51.0 16.9 %copy-start.6 = (s32[256]{0:T(256)S(1)}, s32[256]{0:T(256)}, u32[]{:S(2)}) copy-start(s32[256]{0:T(256)} %param.13) | copy-start | bytes 3076
where the time goes:
time: 69.7 us; the launch traced here: 69.6 us
  blocking collectives  31.4 us (45%)
  Pallas kernels  15.6 us (22%)
  waiting for transfers between devices  13.6 us (20%)
  starting transfers between devices  4.74 us (7%)
  local copies, waits for them, and re-layouts  2.87 us (4%)
  between operations  1.36 us (2%)
    all_to_all x1, blocking collectives, one_round(): got = lax.all_to_all(send, AXES, split_axis=0, concat_axis=0, tiled=True)  31.4 us
    all_to_all x1, waiting for transfers between devices, one_round(): parts = lax.all_to_all(parts, AXES, split_axis=0, concat_axis=0, tiled=True)  13.6 us
    pallas_call x1, Pallas kernels, holder(): pl.pallas_call(holder_kernel, out_shape=jax.ShapeDtypeStruct((DEVS, ROWS,...  8.61 us
    all_to_all x1, starting transfers between devices, one_round(): parts = lax.all_to_all(parts, AXES, split_axis=0, concat_axis=0, tiled=True)  4.65 us
    pallas_call x1, Pallas kernels, suffix(): pl.pallas_call(suffix_kernel, grid=(reqs,), out_shape=(jax.ShapeDtypeStru...  3.28 us
    unnamed x12, local copies, waits for them, and re-layouts  2.36 us
    pallas_call x1, Pallas kernels, route(): pl.pallas_call(functools.partial(route_kernel, offset), out_shape=(jax.Sh...  1.99 us
    pallas_call x1, Pallas kernels, merge(): pl.pallas_call(functools.partial(merge_kernel, len(parts)), out_shape=(ja...  1.75 us
  transfers between devices with their start and end apart: 2, of which 1 were waited for; matrix products, arithmetic and copies ran while one was open for 1% of the time, Pallas kernels for 8%

commit v1 on v0

--- a/solution.py
+++ b/solution.py
@@ -48,14 +48,28 @@
     reqs, blocks = touch.shape
     slots = slot_ref[...]
     chip_of = lax.shift_right_logical(slots, 6) * 16 + (lax.shift_right_logical(slots, 1) & 15)
-    chip_touch = dot(ones_where(iota((chips, blocks), 0) == chip_of), touch, 1, 1)
-    chip_touch = jnp.minimum(chip_touch, 1.0)
+    b = iota((8, blocks), 0)
+    wanted = jnp.where(b < 4, jnp.where(b < 2, me, me ^ 16) * 2 + (b & 1), -1)
+    rows = [ones_where(iota((chips, blocks), 0) == chip_of), ones_where(slots == wanted)]
+    counted = dot(jnp.concatenate(rows, axis=0), touch, 1, 1)
+    chip_touch = jnp.minimum(counted[:chips], 1.0)
+    block_touch = counted[chips:]
+    any_touch = jnp.broadcast_to(jnp.max(block_touch, axis=0, keepdims=True), (8, reqs))
     of_group = lax.shift_right_logical(iota((reqs, reqs), 0), 2)
     before = ones_where(
         (of_group == lax.shift_right_logical(iota((reqs, reqs), 1), 2)) & (iota((reqs, reqs), 0) < iota((reqs, reqs), 1))
     )
-    rank = dot(chip_touch.astype(BF), before)
+    rank = dot(jnp.concatenate([chip_touch, any_touch], axis=0).astype(BF), before)
+    rank, place = rank[:chips], rank[chips:]
     mine = ones_where(iota((reqs, 32), 0) == group * 4 + lax.shift_right_logical(iota((reqs, 32), 1), 3))
+    core = lax.shift_right_logical(me, 4) & 1
+    served = (core ^ (lax.shift_right_logical(iota((8, reqs), 1), 2) & 1)) + offset
+    in_group = ones_where(lax.shift_right_logical(iota((reqs, 128), 0), 2) == iota((reqs, 128), 1))
+    bits = jnp.where(place == served.astype(F32), block_touch, 0.0)
+    sums = dot(jnp.concatenate([chip_touch, bits], axis=0).astype(BF), in_group)
+    bits = sums[chips:]
+    most = jnp.max(jnp.max(sums[:chips], axis=0, keepdims=True), axis=1, keepdims=True)
+    table_ref[...] = jnp.where(iota((8, 128), 0) == 7, most, bits).astype(jnp.int32)
     first = ((group & 1) + offset).astype(F32)
     second = ((1 - (group & 1)) + offset).astype(F32)
     by_core = [jnp.where(rank == want, chip_touch, 0.0) for want in (first, second)]
@@ -75,20 +89,6 @@
     by_place = jnp.concatenate(by_place, axis=1).astype(BF)
     spread = jnp.concatenate(spread, axis=0).astype(BF)
     send_ref[...] = dot(by_place, spread).astype(BF).reshape(send_ref.shape)
-    core = lax.shift_right_logical(me, 4) & 1
-    b = iota((8, blocks), 0)
-    owner = jnp.where(b < 2, me, me ^ 16)
-    wanted = jnp.where(b < 4, owner * 2 + (b & 1), -1)
-    block_touch = dot(ones_where(slots == wanted), touch, 1, 1)
-    any_touch = jnp.max(block_touch, axis=0, keepdims=True)
-    any_touch = jnp.broadcast_to(any_touch, (8, reqs))
-    place = dot(any_touch.astype(BF), before)
-    served = (core ^ (lax.shift_right_logical(iota((8, reqs), 1), 2) & 1)) + offset
-    in_group = ones_where(lax.shift_right_logical(iota((reqs, 128), 0), 2) == iota((reqs, 128), 1))
-    bits = dot(jnp.where(place == served.astype(F32), block_touch, 0.0).astype(BF), in_group)
-    most = dot(chip_touch.astype(BF), in_group)
-    most = jnp.max(jnp.max(most, axis=0, keepdims=True), axis=1, keepdims=True)
-    table_ref[...] = jnp.where(iota((8, 128), 0) == 7, most, bits).astype(jnp.int32)
 
 
 def route(offset, me, q_rows, touch_mask, block_slot):
@@ -140,7 +140,7 @@
         scores = []
         for block, pair in units:
             rows = jnp.concatenate([q[jnp.minimum(g, GROUPS - 1)] for g in pair], axis=0)
-            scores.append(dot(rows, ref[block]))
+            scores.append(dot(rows[:, :LAT], ref[block, :LAT, :]) + dot(rows[:, LAT:], ref[block, LAT:, :]))
         for s, (block, pair) in zip(scores, units):
             old = jnp.concatenate([top[g] for g in pair], axis=0)
             new = jnp.maximum(old, jnp.max(s, axis=1, keepdims=True) * c)

time: 69.7 us -> 68.8 us (0.987)
  transfers between devices with their start and end apart: 2 -> 2, of which waited for: 1 -> 1; matrix products, arithmetic and copies ran while one was open for 1% -> 1% of each run, Pallas kernels for 8% -> 7%
where the time goes in v1:
time: 68.8 us; the launch traced here: 69.3 us
  blocking collectives  31.4 us (46%)
  Pallas kernels  15.2 us (22%)
  waiting for transfers between devices  13.6 us (20%)
  starting transfers between devices  4.74 us (7%)
  local copies, waits for them, and re-layouts  2.87 us (4%)
  between operations  1.38 us (2%)
    all_to_all x1, blocking collectives, one_round(): got = lax.all_to_all(send, AXES, split_axis=0, concat_axis=0, tiled=True)  31.4 us
    all_to_all x1, waiting for transfers between devices, one_round(): parts = lax.all_to_all(parts, AXES, split_axis=0, concat_axis=0, tiled=True)  13.6 us
    pallas_call x1, Pallas kernels, holder(): pl.pallas_call(holder_kernel, out_shape=jax.ShapeDtypeStruct((DEVS, ROWS,...  8.5 us
    all_to_all x1, starting transfers between devices, one_round(): parts = lax.all_to_all(parts, AXES, split_axis=0, concat_axis=0, tiled=True)  4.65 us
    pallas_call x1, Pallas kernels, suffix(): pl.pallas_call(suffix_kernel, grid=(reqs,), out_shape=(jax.ShapeDtypeStru...  3.28 us
    unnamed x12, local copies, waits for them, and re-layouts  2.36 us
    pallas_call x1, Pallas kernels, merge(): pl.pallas_call(functools.partial(merge_kernel, len(parts)), out_shape=(ja...  1.75 us
    pallas_call x1, Pallas kernels, route(): pl.pallas_call(functools.partial(route_kernel, offset), out_shape=(jax.Sh...  1.7 us
  transfers between devices with their start and end apart: 2, of which 1 were waited for; matrix products, arithmetic and copies ran while one was open for 1% of the time, Pallas kernels for 7%

profile of v1, /device:TPU:0, one launch (start us, length us, event | category | flops | bytes accessed | tf_op | source)
XLA Modules:
  0.0 69.3 jit_solution(5479450394340539526)
XLA Ops:
  0.6 0.1 collective-permute-start
  0.7 1.7 %route.3 = (bf16[128,4,1152]{2,1,0:T(4,128)(2,1)S(1)}, bf16[512,32]{1,0:T(8,128)(2,1)S(1)}, s32[8,128]{1,0:T(8,128)S(1)}) custom-call(s32[1]{0:T(128)} %bitcast.1.me_ref, bf16[32,576]{1,0:T(8,128)(2,1)} %bitcast.17, s32[32,256]{1,0:T(8,128)} %touch_ref.1, s32[1,256]{1,0:T(1,128)} %bitcast.19), custom_call_target="tpu_custom_call" | custom-call | flops 33554432 | bytes 1179648 | tf_op jit(solution)/shard_map/route/pallas_call | solution.py:97
  2.4 0.0 copy-start.2
  2.5 31.4 %all_to_all.20.packets_ref = bf16[128,4,1152]{2,1,0:T(4,128)(2,1)S(1)} all-to-all(bf16[128,4,1152]{2,1,0:T(4,128)(2,1)S(1)} %get-tuple-element.53), channel_id=1, replica_groups=mesh['z'=4,'core'=2,'x'=4,'y'=4] {'z','core','x','y'}, dimensions={0} | all-to-all | bytes 2359296 | tf_op jit(solution)/shard_map/all_to_all | solution.py:332
  33.9 0.0 collective-permute-done.far_ref
  33.9 0.0 copy-done.2
  33.9 8.5 %holder.3 = bf16[128,4,1152]{2,1,0:T(4,128)(2,1)} custom-call(s32[8,128]{1,0:T(8,128)S(1)} %get-tuple-element.52.table_ref, bf16[128,4,1152]{2,1,0:T(4,128)(2,1)S(1)} %all_to_all.20.packets_ref, bf16[2,576,1024]{2,1,0:T(8,128)(2,1)S(1)} %bitcast.16, bf16[2,576,1024]{2,1,0:T(8,128)(2,1)} %collective-permute-done.far_ref), custom_call_target="tpu_custom_call" | custom-call | flops 2281701376 | bytes 4718592 | tf_op jit(solution)/shard_map/holder/pallas_call | solution.py:202
  42.4 0.0 copy-start.1
  42.4 0.0 copy-start.4
  42.4 4.6 %all-to-all-start.3 = ((bf16[128,4,1152]{2,1,0:T(4,128)(2,1)}), bf16[128,4,1152]{2,1,0:T(4,128)(2,1)S(1)}, u32[]{:S(2)}, u32[]{:S(2)}) async-start(bf16[128,4,1152]{2,1,0:T(4,128)(2,1)} %holder.3), calls=%async_computation.3 | async-start | bytes 2359296 | tf_op jit(solution)/shard_map/all_to_all | solution.py:334
  47.1 0.5 slice.3
  48.3 0.0 copy-done.1
  48.3 0.0 copy-done.4
  48.3 0.0 copy-start
  48.3 2.3 %copy-done = bf16[4,1024,576]{1,2,0:T(8,128)(2,1)S(1)} copy-done((bf16[4,1024,576]{1,2,0:T(8,128)(2,1)S(1)}, bf16[4,1024,576]{1,2,0:T(8,128)(2,1)}, u32[]{:S(2)}) %copy-start) | copy-done | bytes 4718616
  50.6 0.0 copy-start.5
  50.6 0.0 copy-start.6
  50.6 3.3 %suffix.1 = (f32[4,8,512]{2,1,0:T(8,128)S(1)}, f32[4,8,128]{2,1,0:T(8,128)S(1)}) custom-call(s32[4]{0:T(128)S(1)} %copy-done.1, bf16[4,8,576]{2,1,0:T(8,128)(2,1)S(1)} %copy-done.4, bf16[4,576,1024]{2,1,0:T(8,128)(2,1)S(1)} %bitcast.9), custom_call_target="tpu_custom_call" | custom-call | flops 2281701376 | bytes 4718592 | tf_op jit(solution)/shard_map/suffix/pallas_call | solution.py:240
  53.9 13.6 %all-to-all-done.3 = bf16[128,4,1152]{2,1,0:T(4,128)(2,1)S(1)} async-done(((bf16[128,4,1152]{2,1,0:T(4,128)(2,1)}), bf16[128,4,1152]{2,1,0:T(4,128)(2,1)S(1)}, u32[]{:S(2)}, u32[]{:S(2)}) %all-to-all-start.3) | async-done | bytes 1179680 | tf_op jit(solution)/shard_map/all_to_all | solution.py:334
  67.5 0.0 copy-done.5
  67.5 0.0 copy-done.6
  67.5 1.8 %conditional.1 = ((bf16[4,8,512]{2,1,0:T(8,128)(2,1)}, f32[4,8]{1,0:T(4,128)})) conditional(s32[]{:T(128)} %bitcast.4, (bf16[128,4,1152]{2,1,0:T(4,128)(2,1)S(1)}, bf16[512,32]{1,0:T(8,128)(2,1)S(1)}, f32[32,512]{1,0:T(8,128)S(1)}, f32[32,128]{1,0:T(8,128)S(1)}) %tuple.25, (s32[256]{0:T(256)S(1)}, s32[1]{0:T(128)}, bf16[32,576]{1,0:T(8,128)(2,1)S(1)}, ...), branch_computations={%region_0.0_spmd, %region_1.0_spmd} | conditional | flops 2315255808 | bytes 20054052 | solution.py:349
  67.5 1.8 %merge.2 = (bf16[4,8,512]{2,1,0:T(8,128)(2,1)}, f32[4,8]{1,0:T(4,128)}) custom-call(bf16[128,4,1152]{2,1,0:T(4,128)(2,1)S(1)} %get-tuple-element.28.refs_0_, bf16[512,32]{1,0:T(8,128)(2,1)S(1)} %get-tuple-element.29.refs_1_, f32[32,512]{1,0:T(8,128)S(1)} %get-tuple-element.30.refs_2_, f32[32,128]{1,0:T(8,128)S(1)} %get-tuple-element.31.refs_3_), custom_call_target="tpu_custom_call" | custom-call | tf_op jit(solution)/shard_map/cond/branch_0_fun/merge/pallas_call | solution.py:310
Async XLA Ops:
  0.6 33.3 %collective-permute-start = (bf16[2,576,1024]{2,1,0:T(8,128)(2,1)}, bf16[2,576,1024]{2,1,0:T(8,128)(2,1)}, u32[]{:S(2)}, u32[]{:S(2)}) collective-permute-start(bf16[2,576,1024]{2,1,0:T(8,128)(2,1)} %bitcast.14), channel_id=1, source_target_pairs={{0,16},{16,0},{1,17},{17,1},{2,18},{18,2},{3,19},{19,3},{4,20},{20... | collective-permute-start | bytes 7077896 | tf_op jit(solution)/shard_map/ppermute | solution.py:328
  2.4 31.5 %copy-start.2 = (bf16[2,1024,576]{1,2,0:T(8,128)(2,1)S(1)}, bf16[2,1024,576]{1,2,0:T(8,128)(2,1)}, u32[]{:S(2)}) copy-start(bf16[2,1024,576]{1,2,0:T(8,128)(2,1)} %param.9) | copy-start | bytes 7077892
  42.4 5.9 %copy-start.1 = (s32[4]{0:T(128)S(1)}, s32[4]{0:T(128)}, u32[]{:S(2)}) copy-start(s32[4]{0:T(128)} %len_ref.1) | copy-start | bytes 52
  42.4 5.8 %copy-start.4 = (bf16[4,8,576]{2,1,0:T(8,128)(2,1)S(1)}, bf16[4,8,576]{2,1,0:T(8,128)(2,1)}, u32[]{:S(2)}) copy-start(bf16[4,8,576]{2,1,0:T(8,128)(2,1)} %q_ref.1) | copy-start | bytes 110596
  42.4 25.1 %all-to-all-start.3 = ((bf16[128,4,1152]{2,1,0:T(4,128)(2,1)}), bf16[128,4,1152]{2,1,0:T(4,128)(2,1)S(1)}, u32[]{:S(2)}, u32[]{:S(2)}) async-start(bf16[128,4,1152]{2,1,0:T(4,128)(2,1)} %holder.3), calls=%async_computation.3 | async-start | bytes 2359296 | tf_op jit(solution)/shard_map/all_to_all | solution.py:334
  48.3 2.3 %copy-start = (bf16[4,1024,576]{1,2,0:T(8,128)(2,1)S(1)}, bf16[4,1024,576]{1,2,0:T(8,128)(2,1)}, u32[]{:S(2)}) copy-start(bf16[4,1024,576]{1,2,0:T(8,128)(2,1)} %param.10) | copy-start | bytes 14155780
  50.6 16.9 %copy-start.5 = (s32[32,256]{1,0:T(8,128)S(1)}, s32[32,256]{1,0:T(8,128)}, u32[]{:S(2)}) copy-start(s32[32,256]{1,0:T(8,128)} %touch_ref.1) | copy-start | bytes 98308
  50.6 16.9 %copy-start.6 = (s32[256]{0:T(256)S(1)}, s32[256]{0:T(256)}, u32[]{:S(2)}) copy-start(s32[256]{0:T(256)} %param.13) | copy-start | bytes 3076

commit v2 on v1

--- a/solution.py
+++ b/solution.py
@@ -157,7 +157,17 @@
     for half, ref in enumerate((own_ref, peer_ref)):
         if half == 1:
             fetch.wait()
-        pairs = [lax.shift_right_logical(counts[2 * half + k] + 1, 1) for k in (0, 1)]
+        many = [jnp.where(counts[2 * half + k] >= 7, 1, 0) for k in (0, 1)]
+
+        def wide(block, carry, half=half, ref=ref, many=many):
+            @pl.when(jnp.where(block == 0, many[0], many[1]) == 1)
+            def _():
+                work(ref, [(block, [todo[2 * half + block, 4 * j + k] for k in range(4)]) for j in (0, 1)])
+
+            return carry
+
+        lax.fori_loop(0, 2, wide, 0)
+        pairs = [lax.shift_right_logical(counts[2 * half + k] + 1, 1) * (1 - many[k]) for k in (0, 1)]
         n = pairs[0] + pairs[1]
 
         def unit(u, half=half, pairs=pairs):
@@ -290,8 +300,8 @@
         w = jnp.exp(score - ceiling)
         high = w.astype(BF)
         low = (w - high.astype(F32)).astype(BF)
-        both = jnp.concatenate([high, low], axis=1).T
-        sums = dot(both, part)
+        both = jnp.concatenate([high, low], axis=1)
+        sums = dot(both, part, 0, 0)
         sums = sums[:heads] + sums[heads:]
         total = total + sums[:, SIDE * LAT + 3 * SIDE : SIDE * LAT + 3 * SIDE + 1]
         for j in range(SIDE):

time: 68.8 us -> 68.7 us (level)
  no operation moved by 1% of the time
where the time goes in v2:
time: 68.7 us; the launch traced here: 69.2 us
  blocking collectives  31.4 us (46%)
  Pallas kernels  15.2 us (22%)
  waiting for transfers between devices  13.6 us (20%)
  starting transfers between devices  4.74 us (7%)
  local copies, waits for them, and re-layouts  2.87 us (4%)
  between operations  1.38 us (2%)
    all_to_all x1, blocking collectives, one_round(): got = lax.all_to_all(send, AXES, split_axis=0, concat_axis=0, tiled=True)  31.4 us
    all_to_all x1, waiting for transfers between devices, one_round(): parts = lax.all_to_all(parts, AXES, split_axis=0, concat_axis=0, tiled=True)  13.6 us
    pallas_call x1, Pallas kernels, holder(): pl.pallas_call(holder_kernel, out_shape=jax.ShapeDtypeStruct((DEVS, ROWS,...  8.44 us
    all_to_all x1, starting transfers between devices, one_round(): parts = lax.all_to_all(parts, AXES, split_axis=0, concat_axis=0, tiled=True)  4.65 us
    pallas_call x1, Pallas kernels, suffix(): pl.pallas_call(suffix_kernel, grid=(reqs,), out_shape=(jax.ShapeDtypeStru...  3.28 us
    unnamed x12, local copies, waits for them, and re-layouts  2.36 us
    pallas_call x1, Pallas kernels, merge(): pl.pallas_call(functools.partial(merge_kernel, len(parts)), out_shape=(ja...  1.75 us
    pallas_call x1, Pallas kernels, route(): pl.pallas_call(functools.partial(route_kernel, offset), out_shape=(jax.Sh...  1.7 us
  transfers between devices with their start and end apart: 2, of which 1 were waited for; matrix products, arithmetic and copies ran while one was open for 1% of the time, Pallas kernels for 7%

profile of v2, /device:TPU:0, one launch (start us, length us, event | category | flops | bytes accessed | tf_op | source)
XLA Modules:
  0.0 69.2 jit_solution(15007273675037571716)
XLA Ops:
  0.6 0.1 collective-permute-start
  0.7 1.7 %route.3 = (bf16[128,4,1152]{2,1,0:T(4,128)(2,1)S(1)}, bf16[512,32]{1,0:T(8,128)(2,1)S(1)}, s32[8,128]{1,0:T(8,128)S(1)}) custom-call(s32[1]{0:T(128)} %bitcast.1.me_ref, bf16[32,576]{1,0:T(8,128)(2,1)} %bitcast.17, s32[32,256]{1,0:T(8,128)} %touch_ref.1, s32[1,256]{1,0:T(1,128)} %bitcast.19), custom_call_target="tpu_custom_call" | custom-call | flops 33554432 | bytes 1179648 | tf_op jit(solution)/shard_map/route/pallas_call | solution.py:97
  2.4 0.0 copy-start.2
  2.5 31.4 %all_to_all.20.packets_ref = bf16[128,4,1152]{2,1,0:T(4,128)(2,1)S(1)} all-to-all(bf16[128,4,1152]{2,1,0:T(4,128)(2,1)S(1)} %get-tuple-element.53), channel_id=1, replica_groups=mesh['z'=4,'core'=2,'x'=4,'y'=4] {'z','core','x','y'}, dimensions={0} | all-to-all | bytes 2359296 | tf_op jit(solution)/shard_map/all_to_all | solution.py:342
  33.9 0.0 collective-permute-done.far_ref
  33.9 0.0 copy-done.2
  33.9 8.4 %holder.3 = bf16[128,4,1152]{2,1,0:T(4,128)(2,1)} custom-call(s32[8,128]{1,0:T(8,128)S(1)} %get-tuple-element.52.table_ref, bf16[128,4,1152]{2,1,0:T(4,128)(2,1)S(1)} %all_to_all.20.packets_ref, bf16[2,576,1024]{2,1,0:T(8,128)(2,1)S(1)} %bitcast.16, bf16[2,576,1024]{2,1,0:T(8,128)(2,1)} %collective-permute-done.far_ref), custom_call_target="tpu_custom_call" | custom-call | flops 2281701376 | bytes 4718592 | tf_op jit(solution)/shard_map/holder/pallas_call | solution.py:212
  42.4 0.0 copy-start.1
  42.4 0.0 copy-start.4
  42.4 4.6 %all-to-all-start.3 = ((bf16[128,4,1152]{2,1,0:T(4,128)(2,1)}), bf16[128,4,1152]{2,1,0:T(4,128)(2,1)S(1)}, u32[]{:S(2)}, u32[]{:S(2)}) async-start(bf16[128,4,1152]{2,1,0:T(4,128)(2,1)} %holder.3), calls=%async_computation.3 | async-start | bytes 2359296 | tf_op jit(solution)/shard_map/all_to_all | solution.py:344
  47.0 0.5 slice.3
  48.2 0.0 copy-done.1
  48.2 0.0 copy-done.4
  48.2 0.0 copy-start
  48.2 2.3 %copy-done = bf16[4,1024,576]{1,2,0:T(8,128)(2,1)S(1)} copy-done((bf16[4,1024,576]{1,2,0:T(8,128)(2,1)S(1)}, bf16[4,1024,576]{1,2,0:T(8,128)(2,1)}, u32[]{:S(2)}) %copy-start) | copy-done | bytes 4718616
  50.6 0.0 copy-start.5
  50.6 0.0 copy-start.6
  50.6 3.3 %suffix.1 = (f32[4,8,512]{2,1,0:T(8,128)S(1)}, f32[4,8,128]{2,1,0:T(8,128)S(1)}) custom-call(s32[4]{0:T(128)S(1)} %copy-done.1, bf16[4,8,576]{2,1,0:T(8,128)(2,1)S(1)} %copy-done.4, bf16[4,576,1024]{2,1,0:T(8,128)(2,1)S(1)} %bitcast.9), custom_call_target="tpu_custom_call" | custom-call | flops 2281701376 | bytes 4718592 | tf_op jit(solution)/shard_map/suffix/pallas_call | solution.py:250
  53.9 13.6 %all-to-all-done.3 = bf16[128,4,1152]{2,1,0:T(4,128)(2,1)S(1)} async-done(((bf16[128,4,1152]{2,1,0:T(4,128)(2,1)}), bf16[128,4,1152]{2,1,0:T(4,128)(2,1)S(1)}, u32[]{:S(2)}, u32[]{:S(2)}) %all-to-all-start.3) | async-done | bytes 1179680 | tf_op jit(solution)/shard_map/all_to_all | solution.py:344
  67.5 0.0 copy-done.5
  67.5 0.0 copy-done.6
  67.5 1.8 %conditional.1 = ((bf16[4,8,512]{2,1,0:T(8,128)(2,1)}, f32[4,8]{1,0:T(4,128)})) conditional(s32[]{:T(128)} %bitcast.4, (bf16[128,4,1152]{2,1,0:T(4,128)(2,1)S(1)}, bf16[512,32]{1,0:T(8,128)(2,1)S(1)}, f32[32,512]{1,0:T(8,128)S(1)}, f32[32,128]{1,0:T(8,128)S(1)}) %tuple.25, (s32[256]{0:T(256)S(1)}, s32[1]{0:T(128)}, bf16[32,576]{1,0:T(8,128)(2,1)S(1)}, ...), branch_computations={%region_0.0_spmd, %region_1.0_spmd} | conditional | flops 2315255808 | bytes 20054052 | solution.py:359
  67.5 1.8 %merge.2 = (bf16[4,8,512]{2,1,0:T(8,128)(2,1)}, f32[4,8]{1,0:T(4,128)}) custom-call(bf16[128,4,1152]{2,1,0:T(4,128)(2,1)S(1)} %get-tuple-element.28.refs_0_, bf16[512,32]{1,0:T(8,128)(2,1)S(1)} %get-tuple-element.29.refs_1_, f32[32,512]{1,0:T(8,128)S(1)} %get-tuple-element.30.refs_2_, f32[32,128]{1,0:T(8,128)S(1)} %get-tuple-element.31.refs_3_), custom_call_target="tpu_custom_call" | custom-call | tf_op jit(solution)/shard_map/cond/branch_0_fun/merge/pallas_call | solution.py:320
Async XLA Ops:
  0.6 33.3 %collective-permute-start = (bf16[2,576,1024]{2,1,0:T(8,128)(2,1)}, bf16[2,576,1024]{2,1,0:T(8,128)(2,1)}, u32[]{:S(2)}, u32[]{:S(2)}) collective-permute-start(bf16[2,576,1024]{2,1,0:T(8,128)(2,1)} %bitcast.14), channel_id=1, source_target_pairs={{0,16},{16,0},{1,17},{17,1},{2,18},{18,2},{3,19},{19,3},{4,20},{20... | collective-permute-start | bytes 7077896 | tf_op jit(solution)/shard_map/ppermute | solution.py:338
  2.4 31.5 %copy-start.2 = (bf16[2,1024,576]{1,2,0:T(8,128)(2,1)S(1)}, bf16[2,1024,576]{1,2,0:T(8,128)(2,1)}, u32[]{:S(2)}) copy-start(bf16[2,1024,576]{1,2,0:T(8,128)(2,1)} %param.9) | copy-start | bytes 7077892
  42.4 5.9 %copy-start.1 = (s32[4]{0:T(128)S(1)}, s32[4]{0:T(128)}, u32[]{:S(2)}) copy-start(s32[4]{0:T(128)} %len_ref.1) | copy-start | bytes 52
  42.4 5.8 %copy-start.4 = (bf16[4,8,576]{2,1,0:T(8,128)(2,1)S(1)}, bf16[4,8,576]{2,1,0:T(8,128)(2,1)}, u32[]{:S(2)}) copy-start(bf16[4,8,576]{2,1,0:T(8,128)(2,1)} %q_ref.1) | copy-start | bytes 110596
  42.4 25.1 %all-to-all-start.3 = ((bf16[128,4,1152]{2,1,0:T(4,128)(2,1)}), bf16[128,4,1152]{2,1,0:T(4,128)(2,1)S(1)}, u32[]{:S(2)}, u32[]{:S(2)}) async-start(bf16[128,4,1152]{2,1,0:T(4,128)(2,1)} %holder.3), calls=%async_computation.3 | async-start | bytes 2359296 | tf_op jit(solution)/shard_map/all_to_all | solution.py:344
  48.2 2.3 %copy-start = (bf16[4,1024,576]{1,2,0:T(8,128)(2,1)S(1)}, bf16[4,1024,576]{1,2,0:T(8,128)(2,1)}, u32[]{:S(2)}) copy-start(bf16[4,1024,576]{1,2,0:T(8,128)(2,1)} %param.10) | copy-start | bytes 14155780
  50.6 16.9 %copy-start.5 = (s32[32,256]{1,0:T(8,128)S(1)}, s32[32,256]{1,0:T(8,128)}, u32[]{:S(2)}) copy-start(s32[32,256]{1,0:T(8,128)} %touch_ref.1) | copy-start | bytes 98308
  50.6 16.9 %copy-start.6 = (s32[256]{0:T(256)S(1)}, s32[256]{0:T(256)}, u32[]{:S(2)}) copy-start(s32[256]{0:T(256)} %param.13) | copy-start | bytes 3076
